TPU v7x, 32 devices: a whole 2x2x4 slice. The times are simulated.
32 devices in a mesh: row: 4 (over z), col: 8 (over y, x, core).
Axes of the slice: x: 2, y: 2, z: 4, core: 2. Of those that a mesh axis runs over, the one named last changes fastest.
Arguments:
- query_vectors: bfloat16 [2048, 8, 128], P('col', 'row'), may hold values from -68 to 68
- key_vectors: bfloat16 [2048, 8, 128], P('col', 'row'), may hold values from -6 to 6
- value_vectors: bfloat16 [2048, 8, 128], P('col', 'row'), may hold values from -6 to 6
- gate_logits: bfloat16 [2048, 8, 128], P('col', 'row'), may hold values from -6 to 6
- cotangent: bfloat16 [2048, 8, 128], P('col', 'row'), may hold values from -6 to 6
- pair_bias: bfloat16 [16, 4, 128, 16, 128], P('col'), may hold values from -6 to 6
- block_table: int32 [16, 16], P('col'), may hold values from 0 to 15, as said below
- valid_counts: int32 [16], P('col'), may hold values from 1 to 16
Outputs:
- query_grad: bfloat16 [2048, 8, 128], P('col', 'row')
- key_grad: bfloat16 [2048, 8, 128], P('col', 'row')
- value_grad: bfloat16 [2048, 8, 128], P('col', 'row')
- gate_grad: bfloat16 [2048, 8, 128], P('col', 'row')
- bias_grad: bfloat16 [16, 4, 128, 16, 128], P('col', None, None, 'row')
Inputs may be any that keep to these rules, and one draw needn't show every extreme that they name: `block_table`: each row holds 16 distinct block numbers; its first entry is the row's own block number.
All inputs are finite; a program needn't handle non-finite values.
Results may differ from a plain program's by a relative error of at most 0.03.
Values may be sent and summed in bfloat16 or wider, within the bound.
A program may use at most 128 MiB of HBM per device.

v0:
```python
import functools

import jax
import jax.numpy as jnp
from jax import lax
from jax.experimental import pallas as pl
from jax.experimental.pallas import tpu as pltpu
from jax.sharding import PartitionSpec as P

H = 4
DH = 32
BS = 128
TAB = 16
PAIRS = TAB // 2
C = H * DH
HQ = H * BS
SCALE = DH ** (-0.5)
LOG2E = 1.4426950408889634
F32 = jnp.float32
BF16 = jnp.bfloat16
NT = (((1,), (1,)), ((), ()))
NN = (((1,), (0,)), ((), ()))


def dot(a, b, dims=NN):
    return lax.dot_general(a, b, dims, preferred_element_type=F32)


def attention_kernel(rows, last, *refs):
    (tab_k, tab_v, count, q_ref, g_ref, c_ref, k_ref, v_ref, b_ref), refs = refs[:9], refs[9:]
    if last:
        (dk_in, dv_in), refs = refs[:2], refs[2:]
    (dq_ref, gg_ref, bg_ref, dk_out, dv_out), refs = refs[:5], refs[5:]
    s_ref, e_ref, qm, cm, qt, ct, mx, att, off, dqa = refs[:10]
    if last:
        dk_ref, dv_ref = refs[10:]
        dk_ref[...] = dk_in[...]
        dv_ref[...] = dv_in[...]
    else:
        dk_ref, dv_ref = dk_out, dv_out
        dk_ref[...] = jnp.zeros_like(dk_ref)
        dv_ref[...] = jnp.zeros_like(dv_ref)
    valid = count[0]
    pairs = (valid + 1) // 2
    lane_head = lax.broadcasted_iota(jnp.int32, (BS, C), 1) // DH

    def per_head(x):
        return jnp.concatenate([jnp.where(lane_head == h, x, 0.0) for h in range(H)], 0)

    def merge_heads(x):
        total = jnp.zeros((BS, C), F32)
        for h in range(H):
            total = jnp.where(lane_head == h, x[h * BS : (h + 1) * BS], total)
        return total

    def store_transposed(dst, i, x):
        for hp in range(2):
            turned = jnp.transpose(x[hp * 256 : (hp + 1) * 256])
            dst[i, hp] = turned[hp * 64 : (hp + 1) * 64].astype(BF16)

    def two(ref, tab, p, i):
        lanes = slice(i * C, (i + 1) * C)
        return jnp.concatenate([ref[tab[2 * p], :, lanes], ref[tab[2 * p + 1], :, lanes]], 0)

    def wide(x):
        return jnp.concatenate([x, x], 1)

    for i in range(rows):
        q_heads = per_head(q_ref[:, i * C : (i + 1) * C].astype(F32))
        qm[i] = q_heads.astype(BF16)
        store_transposed(qt, i, q_heads)
        mx[i] = jnp.full((HQ, 128), -jnp.inf, F32)
        att[i] = jnp.zeros((HQ, 256), F32)
        dqa[i] = jnp.zeros((HQ, C), F32)

    @pl.loop(0, pairs)
    def _(p):
        lane_slot = lax.broadcasted_iota(jnp.int32, (1, 2 * BS), 1) // BS
        shut = jnp.where(2 * p + lane_slot < valid, 0.0, -jnp.inf)
        bias = b_ref[p].astype(F32) * LOG2E + shut
        for i in range(rows):
            raw = dot(qm[i], two(k_ref, tab_k, p, i), NT)
            s = raw * (SCALE * LOG2E) + bias
            s_ref[p, i] = s
            mx[i] = jnp.maximum(mx[i], jnp.maximum(s[:, :BS], s[:, BS:]))

    for i in range(rows):
        mx[i] = jnp.broadcast_to(jnp.max(mx[i], axis=1, keepdims=True), (HQ, 128))

    @pl.loop(0, pairs)
    def _(p):
        for i in range(rows):
            e = jnp.exp2(s_ref[p, i] - wide(mx[i])).astype(BF16)
            e_ref[p, i] = e
            values = jnp.concatenate([two(v_ref, tab_v, p, i), jnp.ones((2 * BS, C), BF16)], 1)
            att[i] += dot(e, values)

    for i in range(rows):
        lanes = slice(i * C, (i + 1) * C)
        inverse = 1.0 / att[i, :, C:]
        attended = att[i, :, :C] * inverse
        opened = jax.nn.sigmoid(g_ref[:, lanes].astype(F32))
        upstream = c_ref[:, lanes].astype(F32)
        gg_ref[:, lanes] = (upstream * merge_heads(attended) * opened * (1.0 - opened)).astype(BF16)
        core = (upstream * opened).astype(BF16).astype(F32)
        core_scaled = (per_head(core) * inverse).astype(BF16)
        cm[i] = core_scaled
        scaled = core_scaled.astype(F32)
        store_transposed(ct, i, scaled)
        off[i] = jnp.broadcast_to(jnp.sum(scaled * attended, axis=1, keepdims=True), (HQ, 128))

    @pl.loop(0, pairs)
    def _(p):
        total = None
        for i in range(rows):
            keys = two(k_ref, tab_k, p, i)
            dw = dot(cm[i], two(v_ref, tab_v, p, i), NT)
            e = e_ref[p, i]
            ds = e.astype(F32) * (dw - wide(off[i]))
            total = ds if total is None else total + ds
            half = ds.astype(BF16)
            dqa[i] += dot(half, keys)
            for hp in range(2):
                span = slice(hp * 256, (hp + 1) * 256)
                dst = slice(i * C + hp * 64, i * C + (hp + 1) * 64)
                key_term = dot(qt[i, hp], half[span])
                value_term = dot(ct[i, hp], e[span])
                for slot in range(2):
                    part = slice(slot * BS, (slot + 1) * BS)
                    dk_ref[tab_k[2 * p + slot], dst, :] += key_term[:, part]
                    dv_ref[tab_v[2 * p + slot], dst, :] += value_term[:, part]
        bg_ref[p] = total.astype(BF16)

    @pl.loop(pairs, PAIRS)
    def _(p):
        bg_ref[p] = jnp.zeros((HQ, 2 * BS), BF16)

    for i in range(rows):
        dq_ref[:, i * C : (i + 1) * C] = (merge_heads(dqa[i]) * SCALE).astype(BF16)
    if last:

        @pl.loop(0, dk_ref.shape[0])
        def _(b):
            dk_out[b] = (dk_ref[b] * SCALE).astype(BF16)
            dv_out[b] = dv_ref[b].astype(BF16)


def attention(rows, last, tab_k, tab_v, count, q, g, c, k, v, b, sums):
    blocks = k.shape[0]
    width = rows * C
    smem = pl.BlockSpec(memory_space=pltpu.SMEM)
    vmem = pl.BlockSpec(memory_space=pltpu.VMEM)
    acc = pltpu.VMEM((blocks, width, BS), F32)
    scratch = [
        pltpu.VMEM((PAIRS, rows, HQ, 2 * BS), F32),
        pltpu.VMEM((PAIRS, rows, HQ, 2 * BS), BF16),
        pltpu.VMEM((rows, HQ, C), BF16),
        pltpu.VMEM((rows, HQ, C), BF16),
        pltpu.VMEM((rows, 2, 64, 256), BF16),
        pltpu.VMEM((rows, 2, 64, 256), BF16),
        pltpu.VMEM((rows, HQ, 128), F32),
        pltpu.VMEM((rows, HQ, 256), F32),
        pltpu.VMEM((rows, HQ, 128), F32),
        pltpu.VMEM((rows, HQ, C), F32),
    ]
    sum_type = BF16 if last else F32
    return pl.pallas_call(
        functools.partial(attention_kernel, rows, last),
        out_shape=(
            jax.ShapeDtypeStruct((BS, width), BF16),
            jax.ShapeDtypeStruct((BS, width), BF16),
            jax.ShapeDtypeStruct((PAIRS, HQ, 2 * BS), BF16),
            jax.ShapeDtypeStruct((blocks, width, BS), sum_type),
            jax.ShapeDtypeStruct((blocks, width, BS), sum_type),
        ),
        in_specs=[smem] * 3 + [vmem] * (6 + len(sums)),
        out_specs=[vmem] * 5,
        scratch_shapes=scratch + ([acc, acc] if last else []),
        compiler_params=pltpu.CompilerParams(vmem_limit_bytes=56 * 1024 * 1024),
        cost_estimate=pl.CostEstimate(
            flops=6 * 2 * rows * HQ * TAB * BS * 256,
            bytes_accessed=12 * 1024 * 1024,
            transcendentals=rows * HQ * TAB * BS,
        ),
    )(tab_k, tab_v, count, q, g, c, k, v, b, *sums)


def exchange(x, bit, size):
    return lax.ppermute(x, "col", [(d, d ^ bit) for d in range(size)])


def gather(x, order, size):
    for bit in order:
        x = jnp.concatenate([x, exchange(x, bit, size)], 0)
    return x


def scatter_sum(x, order, size):
    for bit in reversed(order):
        half = x.shape[0] // 2
        got = exchange(x[half:], bit, size)
        x = (x[:half].astype(F32) + got.astype(F32)).astype(BF16)
    return x


def positions(blocks, order, me, per_device):
    apart = (blocks // per_device) ^ me
    place = jnp.zeros_like(apart)
    for rank, bit in enumerate(order):
        place = place + jnp.where((apart & bit) != 0, 1 << rank, 0)
    return place * per_device + blocks % per_device


def body(q, k, v, g, c, pair_bias, block_table, valid_counts):
    length, rows, channels = q.shape
    local = length // BS
    width = rows * channels
    size = lax.axis_size("col")
    me = lax.axis_index("col")
    bits = [1 << n for n in range(size.bit_length() - 1)]
    order_k = bits[1:] + bits[:1]
    order_v = bits[1:][::-1] + bits[:1]
    k_all = gather(k.reshape(local, BS, width), order_k, size)
    v_all = gather(v.reshape(local, BS, width), order_v, size)
    tab_k = positions(block_table, order_k, me, local)
    tab_v = positions(block_table, order_v, me, local)
    q, g, c = (x.reshape(local, BS, width) for x in (q, g, c))
    bias = pair_bias.reshape(local, HQ, PAIRS, 2 * BS).transpose(0, 2, 1, 3)
    sums = ()
    dqs, ggs, biases = [], [], []
    for j in range(local):
        dq, gg, bg, *sums = attention(
            rows, j == local - 1, tab_k[j], tab_v[j], valid_counts[j : j + 1],
            q[j], g[j], c[j], k_all, v_all, bias[j], sums,
        )
        dqs.append(dq)
        ggs.append(gg)
        biases.append(lax.psum_scatter(bg, "row", scatter_dimension=0, tiled=True))
    dk = scatter_sum(sums[0], order_k, size)
    dv = scatter_sum(sums[1], order_v, size)

    def leave(x):
        return x.transpose(0, 2, 1).reshape(length, rows, channels)

    own = biases[0].shape[0]
    bias_grad = jnp.stack(biases, 0).reshape(local, own, H, BS, 2, BS)
    bias_grad = bias_grad.transpose(0, 2, 3, 1, 4, 5).reshape(local, H, BS, own * 2, BS)
    return (
        jnp.concatenate(dqs, 0).reshape(length, rows, channels),
        leave(dk),
        leave(dv),
        jnp.concatenate(ggs, 0).reshape(length, rows, channels),
        bias_grad,
    )


def solution(mesh):
    split = P("col", "row", None)
    bias = P("col", None, None, None, None)
    return jax.shard_map(
        body,
        mesh=mesh,
        in_specs=(split,) * 5 + (bias, P("col", None), P("col")),
        out_specs=(split,) * 4 + (P("col", None, None, "row", None),),
        check_vma=False,
    )
```

profile of v0, /device:TPU:18, one launch (start us, length us, event | category | flops | bytes accessed | tf_op | source)
XLA Modules:
  0.0 173.7 jit_solution(2352274183225340591)
XLA Ops:
  7.2 1.0 reshape.55
  8.2 1.6 collective-permute-start.3
  9.8 1.0 reshape.54
  10.8 0.6 collective-permute-start
  11.4 0.7 multiply_add_fusion
  12.1 0.6 slice_bitcast_fusion.4
  12.7 0.7 multiply_add_fusion.1
  13.4 1.0 fusion.6
  14.3 1.0 fusion.5
  15.3 1.0 fusion.4
  16.3 7.1 %reshape.56 = bf16[2,512,8,256]{3,2,1,0:T(8,128)(2,1)} reshape(bf16[2,4,128,16,128]{4,3,2,1,0:T(8,128)(2,1)} %param.13) | data formatting | bytes 8388608 | tf_op jit(solution)/shard_map/reshape | solution.py:228
  23.3 3.1 %copy.31 = bf16[2,512,8,256]{3,1,2,0:T(8,128)(2,1)S(1)} copy(bf16[2,512,8,256]{3,2,1,0:T(8,128)(2,1)} %reshape.56) | data formatting | bytes 8388608 | tf_op jit(solution)/shard_map/reshape | solution.py:228
  26.5 2.3 %slice_bitcast_fusion.1 = (bf16[8,512,256]{2,1,0:T(8,128)(2,1)}, bf16[8,512,256]{2,1,0:T(8,128)(2,1)}) fusion(bf16[2,8,512,256]{3,2,1,0:T(8,128)(2,1)S(1)} %bitcast.48), kind=kLoop, calls=%fused_computation.2 | loop fusion | bytes 8388608 | tf_op jit(solution)/shard_map/squeeze | solution.py:234
  28.8 0.6 slice_bitcast_fusion.5
  29.5 1.6 collective-permute-start.4
  31.0 0.6 collective-permute-start.1
  31.6 0.6 fusion.7
  32.2 0.6 copy.37
  32.9 0.6 copy.34
  33.5 0.6 copy.36
  34.1 0.6 copy.33
  34.8 0.6 copy.35
  35.4 0.6 copy.32
  36.1 0.9 collective-permute-done.4
  37.0 0.1 pad_maximum_fusion.1
  37.1 0.1 collective-permute-start.5
  37.1 1.2 collective-permute-done.1
  38.3 0.1 pad_maximum_fusion
  38.4 0.1 collective-permute-start.2
  38.5 0.5 collective-permute-done.5
  39.1 1.3 collective-permute-done.2
  40.4 1.0 copy-done.7
  41.4 15.2 %shard_map.119 = (bf16[128,256]{1,0:T(8,128)(2,1)}, bf16[128,256]{1,0:T(8,128)(2,1)}, bf16[8,512,256]{2,1,0:T(8,128)(2,1)}, f32[16,256,128]{2,1,0:T(8,128)}, f32[16,256,128]{2,1,0:T(8,128)}) custom-call(s32[16]{0:T(128)} %get-tuple-element.37.refs_0_, s32[16]{0:T(128)} %get-tuple-element.35.refs_1_, s32[1]{0:T(128)} %get-tuple-element.39.refs_2_, ...), custom_call_target="tpu_custom_call" | custom-call | flops 6442450944 | bytes 12582912 | tf_op jit(solution)/shard_map/pallas_call | solution.py:167
  56.6 9.2 %shard_map.120 = (bf16[128,256]{1,0:T(8,128)(2,1)}, bf16[128,256]{1,0:T(8,128)(2,1)}, bf16[8,512,256]{2,1,0:T(8,128)(2,1)}, bf16[16,256,128]{2,1,0:T(8,128)(2,1)}, bf16[16,256,128]{2,1,0:T(8,128)(2,1)}) custom-call(s32[16]{0:T(128)} %get-tuple-element.38.refs_0_, s32[16]{0:T(128)} %get-tuple-element.36.refs_1_, s32[1]{0:T(128)} %get-tuple-element.40.refs_2_, ...), custom_call_target="tpu_custom_call" | custom-call | flops 6442450944 | bytes 12582912 | tf_op jit(solution)/shard_map/pallas_call | solution.py:167
  65.8 0.2 reduce-scatter.3.cloned.1.call-start
  66.0 0.5 reduce-scatter.3.cloned.1.call-update
  66.5 0.4 copy-done.1
  67.0 3.0 %collective-permute-start.9 = (bf16[8,256,128]{2,1,0:T(8,128)(2,1)S(1)}, bf16[8,256,128]{2,1,0:T(8,128)(2,1)S(1)}, u32[]{:S(2)}, u32[]{:S(2)}) collective-permute-start(bf16[8,256,128]{2,1,0:T(8,128)(2,1)S(1)} %slice.105), channel_id=1, source_target_pairs={{0,1},{1,0},{2,3},{3,2},{4,5},{5,4},{6,7},{7,6},{8,9},{9,8},{10,11... | collective-permute-start | bytes 1572872 | tf_op jit(solution)/shard_map/ppermute | solution.py:189
  70.1 0.3 collective-permute-start.6
  70.3 1.2 collective-permute-done.9
  71.5 0.1 add_convert_fusion
  71.7 6.5 %collective-permute-start.10 = (bf16[4,256,128]{2,1,0:T(8,128)(2,1)S(1)}, bf16[4,256,128]{2,1,0:T(8,128)(2,1)S(1)}, u32[]{:S(2)}, u32[]{:S(2)}) collective-permute-start(bf16[4,256,128]{2,1,0:T(8,128)(2,1)S(1)} %slice.117), channel_id=1, source_target_pairs={{0,2},{1,3},{2,0},{3,1},{4,6},{5,7},{6,4},{7,5},{8,10},{9,11},{10,... | collective-permute-start | bytes 786440 | tf_op jit(solution)/shard_map/ppermute | solution.py:189
  78.2 0.1 add_convert_fusion.1
  78.4 0.1 collective-permute-start.7
  78.6 0.7 reshape.57
  79.2 0.7 reshape.60
  79.9 5.1 %collective-permute-done.10 = bf16[4,256,128]{2,1,0:T(8,128)(2,1)S(1)} collective-permute-done((bf16[4,256,128]{2,1,0:T(8,128)(2,1)S(1)}, bf16[4,256,128]{2,1,0:T(8,128)(2,1)S(1)}, u32[]{:S(2)}, u32[]{:S(2)}) %collective-permute-start.10) | collective-permute-done | bytes 262176 | tf_op jit(solution)/shard_map/ppermute | solution.py:189
  85.1 0.1 add_convert_fusion.2
  85.2 0.1 collective-permute-start.11
  85.2 1.5 collective-permute-done.7
  86.8 0.1 add_convert_fusion.3
  86.9 0.9 collective-permute-start.8
  87.7 2.8 %collective-permute-done.11 = bf16[2,256,128]{2,1,0:T(8,128)(2,1)S(1)} collective-permute-done((bf16[2,256,128]{2,1,0:T(8,128)(2,1)S(1)}, bf16[2,256,128]{2,1,0:T(8,128)(2,1)S(1)}, u32[]{:S(2)}, u32[]{:S(2)}) %collective-permute-start.11) | collective-permute-done | bytes 131104 | tf_op jit(solution)/shard_map/ppermute | solution.py:189
  90.6 0.1 copy.16
  90.7 0.7 reshape.59
  91.4 0.5 collective-permute-done.8
  91.9 0.1 copy.15
  92.1 0.7 reshape.58
  92.7 24.0 %reduce-scatter.5.cloned.1.call-done = bf16[2,512,256]{2,1,0:T(8,128)(2,1)} async-done(((bf16[8,512,256]{2,1,0:T(8,128)(2,1)}), bf16[2,512,256]{2,1,0:T(8,128)(2,1)}) %reduce-scatter.5.cloned.1.call-update) | async-done | bytes 524304 | tf_op jit(solution)/shard_map/reduce_scatter | solution.py:238
  116.7 1.2 stack.10
  117.9 44.5 %reduce-scatter.3.cloned.1.call-done = bf16[2,512,256]{2,1,0:T(8,128)(2,1)} async-done(((bf16[8,512,256]{2,1,0:T(8,128)(2,1)}), bf16[2,512,256]{2,1,0:T(8,128)(2,1)}) %reduce-scatter.3.cloned.1.call-update) | async-done | bytes 524304 | tf_op jit(solution)/shard_map/reduce_scatter | solution.py:238
  162.4 1.2 stack.9
  163.5 1.5 maximum_bitcast_fusion
  165.0 1.8 %copy.17 = bf16[2,4,128,2,2,128]{5,4,3,2,1,0:T(2,128)(2,1)} copy(bf16[2,4,128,2,2,128]{5,4,2,1,3,0:T(2,128)(2,1)S(1)} %maximum_bitcast_fusion) | data formatting | bytes 2097152 | tf_op jit(solution)/shard_map/transpose | solution.py:247
  (40 shorter events, 0.5 us)
Async XLA Ops:
  7.2 109.6 %reduce-scatter.5.cloned.1.call-start = ((), (), s32[]{:S(2)}) async-start(), calls=%async_computation.3 | async-start | bytes 2621440 | tf_op jit(solution)/shard_map/reduce_scatter | solution.py:238
  8.2 21.2 %collective-permute-start.3 = (bf16[2,128,256]{2,1,0:T(8,128)(2,1)S(1)}, bf16[2,128,256]{2,1,0:T(8,128)(2,1)S(1)}, u32[]{:S(2)}, u32[]{:S(2)}) collective-permute-start(bf16[2,128,256]{2,1,0:T(8,128)(2,1)S(1)} %reshape.55), channel_id=1, source_target_pairs={{0,4},{1,5},{2,6},{3,7},{4,0},{5,1},{6,2},{7,3},{8,12},{9,13},{10,... | collective-permute-start | bytes 393224 | tf_op jit(solution)/shard_map/ppermute | solution.py:189
  10.8 20.2 %collective-permute-start = (bf16[2,128,256]{2,1,0:T(8,128)(2,1)S(1)}, bf16[2,128,256]{2,1,0:T(8,128)(2,1)S(1)}, u32[]{:S(2)}, u32[]{:S(2)}) collective-permute-start(bf16[2,128,256]{2,1,0:T(8,128)(2,1)S(1)} %reshape.54), channel_id=1, source_target_pairs={{0,2},{1,3},{2,0},{3,1},{4,6},{5,7},{6,4},{7,5},{8,10},{9,11},{10,... | collective-permute-start | bytes 393224 | tf_op jit(solution)/shard_map/ppermute | solution.py:189
  26.5 5.1 %copy-start.8 = (s32[2]{0:T(128)S(1)}, s32[2]{0:T(128)}, u32[]{:S(2)}) copy-start(s32[2]{0:T(128)} %param.15) | copy-start | bytes 28
  29.5 7.6 %collective-permute-start.4 = (bf16[4,128,256]{2,1,0:T(8,128)(2,1)S(1)}, bf16[4,128,256]{2,1,0:T(8,128)(2,1)S(1)}, u32[]{:S(2)}, u32[]{:S(2)}) collective-permute-start(bf16[4,128,256]{2,1,0:T(8,128)(2,1)S(1)} %pad_maximum_fusion.3), channel_id=1, source_target_pairs={{0,2},{1,3},{2,0},{3,1},{4,6},{5,7},{6,4},{7,5},{8,10},{9,11},{10,... | collective-permute-start | bytes 786440 | tf_op jit(solution)/shard_map/ppermute | solution.py:189
  31.0 7.3 %collective-permute-start.1 = (bf16[4,128,256]{2,1,0:T(8,128)(2,1)S(1)}, bf16[4,128,256]{2,1,0:T(8,128)(2,1)S(1)}, u32[]{:S(2)}, u32[]{:S(2)}) collective-permute-start(bf16[4,128,256]{2,1,0:T(8,128)(2,1)S(1)} %pad_maximum_fusion.2), channel_id=1, source_target_pairs={{0,4},{1,5},{2,6},{3,7},{4,0},{5,1},{6,2},{7,3},{8,12},{9,13},{10,... | collective-permute-start | bytes 786440 | tf_op jit(solution)/shard_map/ppermute | solution.py:189
  37.1 2.0 %collective-permute-start.5 = (bf16[8,128,256]{2,1,0:T(8,128)(2,1)S(1)}, bf16[8,128,256]{2,1,0:T(8,128)(2,1)S(1)}, u32[]{:S(2)}, u32[]{:S(2)}) collective-permute-start(bf16[8,128,256]{2,1,0:T(8,128)(2,1)S(1)} %pad_maximum_fusion.1), channel_id=1, source_target_pairs={{0,1},{1,0},{2,3},{3,2},{4,5},{5,4},{6,7},{7,6},{8,9},{9,8},{10,11... | collective-permute-start | bytes 1572872 | tf_op jit(solution)/shard_map/ppermute | solution.py:189
  38.4 2.0 %collective-permute-start.2 = (bf16[8,128,256]{2,1,0:T(8,128)(2,1)S(1)}, bf16[8,128,256]{2,1,0:T(8,128)(2,1)S(1)}, u32[]{:S(2)}, u32[]{:S(2)}) collective-permute-start(bf16[8,128,256]{2,1,0:T(8,128)(2,1)S(1)} %pad_maximum_fusion), channel_id=1, source_target_pairs={{0,1},{1,0},{2,3},{3,2},{4,5},{5,4},{6,7},{7,6},{8,9},{9,8},{10,11... | collective-permute-start | bytes 1572872 | tf_op jit(solution)/shard_map/ppermute | solution.py:189
  39.1 1.3 copy-start.6
  40.4 1.0 copy-start.7
  65.7 1.2 copy-start.1
  65.8 4.2 %copy-start = (bf16[16,256,128]{2,1,0:T(8,128)(2,1)S(1)}, bf16[16,256,128]{2,1,0:T(8,128)(2,1)}, u32[]{:S(2)}) copy-start(bf16[16,256,128]{2,1,0:T(8,128)(2,1)} %get-tuple-element.19) | copy-start | bytes 3145732
  65.8 96.6 %reduce-scatter.3.cloned.1.call-start = ((), (), s32[]{:S(2)}) async-start(), calls=%async_computation.2 | async-start | bytes 2621440 | tf_op jit(solution)/shard_map/reduce_scatter | solution.py:238
  67.0 4.5 %collective-permute-start.9 = (bf16[8,256,128]{2,1,0:T(8,128)(2,1)S(1)}, bf16[8,256,128]{2,1,0:T(8,128)(2,1)S(1)}, u32[]{:S(2)}, u32[]{:S(2)}) collective-permute-start(bf16[8,256,128]{2,1,0:T(8,128)(2,1)S(1)} %slice.105), channel_id=1, source_target_pairs={{0,1},{1,0},{2,3},{3,2},{4,5},{5,4},{6,7},{7,6},{8,9},{9,8},{10,11... | collective-permute-start | bytes 1572872 | tf_op jit(solution)/shard_map/ppermute | solution.py:189
  70.0 8.5 %copy-start.2 = (bf16[128,256]{1,0:T(8,128)(2,1)S(1)}, bf16[128,256]{1,0:T(8,128)(2,1)}, u32[]{:S(2)}) copy-start(bf16[128,256]{1,0:T(8,128)(2,1)} %get-tuple-element.15) | copy-start | bytes 196612
  70.0 8.5 %copy-start.3 = (bf16[128,256]{1,0:T(8,128)(2,1)S(1)}, bf16[128,256]{1,0:T(8,128)(2,1)}, u32[]{:S(2)}) copy-start(bf16[128,256]{1,0:T(8,128)(2,1)} %get-tuple-element.21) | copy-start | bytes 196612
  70.0 8.5 %copy-start.4 = (bf16[128,256]{1,0:T(8,128)(2,1)S(1)}, bf16[128,256]{1,0:T(8,128)(2,1)}, u32[]{:S(2)}) copy-start(bf16[128,256]{1,0:T(8,128)(2,1)} %get-tuple-element.18) | copy-start | bytes 196612
  70.1 8.5 %copy-start.5 = (bf16[128,256]{1,0:T(8,128)(2,1)S(1)}, bf16[128,256]{1,0:T(8,128)(2,1)}, u32[]{:S(2)}) copy-start(bf16[128,256]{1,0:T(8,128)(2,1)} %get-tuple-element.22) | copy-start | bytes 196612
  70.1 8.2 %collective-permute-start.6 = (bf16[8,256,128]{2,1,0:T(8,128)(2,1)S(1)}, bf16[8,256,128]{2,1,0:T(8,128)(2,1)S(1)}, u32[]{:S(2)}, u32[]{:S(2)}) collective-permute-start(bf16[8,256,128]{2,1,0:T(8,128)(2,1)S(1)} %slice.99), channel_id=1, source_target_pairs={{0,1},{1,0},{2,3},{3,2},{4,5},{5,4},{6,7},{7,6},{8,9},{9,8},{10,11... | collective-permute-start | bytes 1572872 | tf_op jit(solution)/shard_map/ppermute | solution.py:189
  71.7 13.4 %collective-permute-start.10 = (bf16[4,256,128]{2,1,0:T(8,128)(2,1)S(1)}, bf16[4,256,128]{2,1,0:T(8,128)(2,1)S(1)}, u32[]{:S(2)}, u32[]{:S(2)}) collective-permute-start(bf16[4,256,128]{2,1,0:T(8,128)(2,1)S(1)} %slice.117), channel_id=1, source_target_pairs={{0,2},{1,3},{2,0},{3,1},{4,6},{5,7},{6,4},{7,5},{8,10},{9,11},{10,... | collective-permute-start | bytes 786440 | tf_op jit(solution)/shard_map/ppermute | solution.py:189
  78.4 8.4 %collective-permute-start.7 = (bf16[4,256,128]{2,1,0:T(8,128)(2,1)S(1)}, bf16[4,256,128]{2,1,0:T(8,128)(2,1)S(1)}, u32[]{:S(2)}, u32[]{:S(2)}) collective-permute-start(bf16[4,256,128]{2,1,0:T(8,128)(2,1)S(1)} %slice.113), channel_id=1, source_target_pairs={{0,4},{1,5},{2,6},{3,7},{4,0},{5,1},{6,2},{7,3},{8,12},{9,13},{10,... | collective-permute-start | bytes 786440 | tf_op jit(solution)/shard_map/ppermute | solution.py:189
  85.2 5.4 %collective-permute-start.11 = (bf16[2,256,128]{2,1,0:T(8,128)(2,1)S(1)}, bf16[2,256,128]{2,1,0:T(8,128)(2,1)S(1)}, u32[]{:S(2)}, u32[]{:S(2)}) collective-permute-start(bf16[2,256,128]{2,1,0:T(8,128)(2,1)S(1)} %slice.119), channel_id=1, source_target_pairs={{0,4},{1,5},{2,6},{3,7},{4,0},{5,1},{6,2},{7,3},{8,12},{9,13},{10,... | collective-permute-start | bytes 393224 | tf_op jit(solution)/shard_map/ppermute | solution.py:189
  86.9 5.0 %collective-permute-start.8 = (bf16[2,256,128]{2,1,0:T(8,128)(2,1)S(1)}, bf16[2,256,128]{2,1,0:T(8,128)(2,1)S(1)}, u32[]{:S(2)}, u32[]{:S(2)}) collective-permute-start(bf16[2,256,128]{2,1,0:T(8,128)(2,1)S(1)} %slice.115), channel_id=1, source_target_pairs={{0,2},{1,3},{2,0},{3,1},{4,6},{5,7},{6,4},{7,5},{8,10},{9,11},{10,... | collective-permute-start | bytes 393224 | tf_op jit(solution)/shard_map/ppermute | solution.py:189
Sparse Core Ops, SparseCore 0:
  65.9 50.8 reduce-scatter.4
  119.1 43.1 reduce-scatter.2
where the time goes:
time: 176 us; the launch traced here: 174 us
  waiting for transfers between devices  84 us (48%)
  local copies, waits for them, and re-layouts  31.8 us (18%)
  Pallas kernels  24.4 us (14%)
  starting transfers between devices  15.5 us (9%)
  between operations  14.4 us (8%)
  other arithmetic  3.54 us (2%)
    reduce_scatter x2, waiting for transfers between devices, body(): biases.append(lax.psum_scatter(bg, 'row', scatter_dimension=0, tiled=True))  68.5 us
    pallas_call x2, Pallas kernels, attention(): pl.pallas_call(functools.partial(attention_kernel, rows, last), out_shape...  24.4 us
    ppermute x12, starting transfers between devices, exchange(): return lax.ppermute(x, 'col', [(d, d ^ bit) for d in range(size)])  15.3 us
    ppermute x12, waiting for transfers between devices, exchange(): return lax.ppermute(x, 'col', [(d, d ^ bit) for d in range(size)])  15 us
    reshape x2, local copies, waits for them, and re-layouts, body(): bias = pair_bias.reshape(local, HQ, PAIRS, 2 * BS).transpose(0, 2, 1, 3)  10.2 us
    unnamed x30, local copies, waits for them, and re-layouts  5.34 us
  transfers between devices with their start and end apart: 14, of which 11 were waited for; matrix products, arithmetic and copies ran while one was open for 16% of the time, Pallas kernels for 0%

commit v1 on v0

--- a/solution.py
+++ b/solution.py
@@ -31,9 +31,9 @@
     if last:
         (dk_in, dv_in), refs = refs[:2], refs[2:]
     (dq_ref, gg_ref, bg_ref, dk_out, dv_out), refs = refs[:5], refs[5:]
-    s_ref, e_ref, qm, cm, qt, ct, mx, att, off, dqa = refs[:10]
+    s_ref, e_ref, qm, cm, qt, ct, mx, att, off, dqa, bias_ref = refs[:11]
     if last:
-        dk_ref, dv_ref = refs[10:]
+        dk_ref, dv_ref = refs[11:]
         dk_ref[...] = dk_in[...]
         dv_ref[...] = dv_in[...]
     else:
@@ -65,6 +65,10 @@
     def wide(x):
         return jnp.concatenate([x, x], 1)
 
+    for h in range(H):
+        span = slice(h * BS * TAB, (h + 1) * BS * TAB)
+        bias_ref[span] = b_ref[h].reshape(BS * TAB, BS).astype(F32) * LOG2E
+
     for i in range(rows):
         q_heads = per_head(q_ref[:, i * C : (i + 1) * C].astype(F32))
         qm[i] = q_heads.astype(BF16)
@@ -77,7 +81,9 @@
     def _(p):
         lane_slot = lax.broadcasted_iota(jnp.int32, (1, 2 * BS), 1) // BS
         shut = jnp.where(2 * p + lane_slot < valid, 0.0, -jnp.inf)
-        bias = b_ref[p].astype(F32) * LOG2E + shut
+        first = bias_ref[pl.ds(2 * p, HQ, stride=TAB), :]
+        second = bias_ref[pl.ds(2 * p + 1, HQ, stride=TAB), :]
+        bias = jnp.concatenate([first, second], 1) + shut
         for i in range(rows):
             raw = dot(qm[i], two(k_ref, tab_k, p, i), NT)
             s = raw * (SCALE * LOG2E) + bias
@@ -145,11 +151,13 @@
             dv_out[b] = dv_ref[b].astype(BF16)
 
 
-def attention(rows, last, tab_k, tab_v, count, q, g, c, k, v, b, sums):
+def attention(rows, j, last, tab_k, tab_v, count, q, g, c, k, v, b, sums):
     blocks = k.shape[0]
     width = rows * C
     smem = pl.BlockSpec(memory_space=pltpu.SMEM)
     vmem = pl.BlockSpec(memory_space=pltpu.VMEM)
+    block = pl.BlockSpec((None, BS, width), lambda n: (j, 0, 0))
+    bias_block = pl.BlockSpec((None, H, BS, TAB, BS), lambda n: (j, 0, 0, 0, 0))
     acc = pltpu.VMEM((blocks, width, BS), F32)
     scratch = [
         pltpu.VMEM((PAIRS, rows, HQ, 2 * BS), F32),
@@ -162,6 +170,7 @@
         pltpu.VMEM((rows, HQ, 256), F32),
         pltpu.VMEM((rows, HQ, 128), F32),
         pltpu.VMEM((rows, HQ, C), F32),
+        pltpu.VMEM((HQ * TAB, BS), F32),
     ]
     sum_type = BF16 if last else F32
     return pl.pallas_call(
@@ -173,7 +182,8 @@
             jax.ShapeDtypeStruct((blocks, width, BS), sum_type),
             jax.ShapeDtypeStruct((blocks, width, BS), sum_type),
         ),
-        in_specs=[smem] * 3 + [vmem] * (6 + len(sums)),
+        grid=(1,),
+        in_specs=[smem] * 3 + [block] * 3 + [vmem] * 2 + [bias_block] + [vmem] * len(sums),
         out_specs=[vmem] * 5,
         scratch_shapes=scratch + ([acc, acc] if last else []),
         compiler_params=pltpu.CompilerParams(vmem_limit_bytes=56 * 1024 * 1024),
@@ -201,6 +211,29 @@
         got = exchange(x[half:], bit, size)
         x = (x[:half].astype(F32) + got.astype(F32)).astype(BF16)
     return x
+
+
+def line_sum(x):
+    size = lax.axis_size("row")
+    me = lax.axis_index("row")
+    share = x.shape[0] // size
+
+    def own(owner):
+        start = jnp.clip(owner, 0, size - 1) * share
+        return lax.dynamic_slice_in_dim(x, start, share, 0).astype(F32)
+
+    down = up = None
+    for step in range(size - 1):
+        down_term = own(me + step - (size - 1))
+        up_term = own(me + (size - 1) - step)
+        if step > 0:
+            down_term = down_term + down.astype(F32)
+            up_term = up_term + up.astype(F32)
+        down_pairs = [(r, r - 1) for r in range(max(1, size - 1 - step), size)]
+        up_pairs = [(r, r + 1) for r in range(min(size - 1, step + 1))]
+        down = lax.ppermute(down_term.astype(BF16), "row", down_pairs)
+        up = lax.ppermute(up_term.astype(BF16), "row", up_pairs)
+    return (own(me) + down.astype(F32) + up.astype(F32)).astype(BF16)
 
 
 def positions(blocks, order, me, per_device):
@@ -225,17 +258,17 @@
     tab_k = positions(block_table, order_k, me, local)
     tab_v = positions(block_table, order_v, me, local)
     q, g, c = (x.reshape(local, BS, width) for x in (q, g, c))
-    bias = pair_bias.reshape(local, HQ, PAIRS, 2 * BS).transpose(0, 2, 1, 3)
     sums = ()
-    dqs, ggs, biases = [], [], []
+    dqs, ggs, terms = [], [], []
     for j in range(local):
         dq, gg, bg, *sums = attention(
-            rows, j == local - 1, tab_k[j], tab_v[j], valid_counts[j : j + 1],
-            q[j], g[j], c[j], k_all, v_all, bias[j], sums,
+            rows, j, j == local - 1, tab_k[j], tab_v[j], valid_counts[j : j + 1],
+            q, g, c, k_all, v_all, pair_bias, sums,
         )
         dqs.append(dq)
         ggs.append(gg)
-        biases.append(lax.psum_scatter(bg, "row", scatter_dimension=0, tiled=True))
+        terms.append(bg)
+    biases = [line_sum(bg) for bg in terms]
     dk = scatter_sum(sums[0], order_k, size)
     dv = scatter_sum(sums[1], order_v, size)
 

time: 176 us -> 154 us (0.88); the launches traced: 174 us -> 157 us
  waiting for transfers between devices: 84 us -> 53.1 us
  Pallas kernels: 24.4 us -> 38.7 us
  between operations: 14.4 us -> 1.15 us
  starting transfers between devices: 15.5 us -> 28.3 us
  other arithmetic: 3.54 us -> 14.9 us
  local copies, waits for them, and re-layouts: 31.8 us -> 20.6 us
    reduce_scatter x2 -> x0, waiting for transfers between devices: 68.5 us -> none  [body(): biases.append(lax.psum_scatter(bg, 'row', scatter_dimension=0, tiled=True))]
    ppermute x0 -> x12, waiting for transfers between devices: none -> 49.2 us  [the longest x6 25.8 us: line_sum(): up = lax.ppermute(up_term.astype(BF16), 'row', up_pairs)]
    ppermute x0 -> x12, starting transfers between devices: none -> 23 us  [the longest x6 14.1 us: line_sum(): down = lax.ppermute(down_term.astype(BF16), 'row', down_pairs)]
    pallas_call x2, Pallas kernels: 24.4 us -> 38.7 us  [attention(): pl.pallas_call(functools.partial(attention_kernel, rows, last), out_shape...]
    ppermute x12, waiting for transfers between devices: 15 us -> 3.85 us  [exchange(): return lax.ppermute(x, 'col', [(d, d ^ bit) for d in range(size)])]
    convert_element_type x0 -> x8, other arithmetic: none -> 10.3 us  [the longest x4 5.56 us: line_sum(): down = lax.ppermute(down_term.astype(BF16), 'row', down_pairs)]
    ppermute x12, starting transfers between devices: 15.3 us -> 5.24 us  [exchange(): return lax.ppermute(x, 'col', [(d, d ^ bit) for d in range(size)])]
    reshape x2 -> x3, local copies, waits for them, and re-layouts: 10.2 us -> 3.14 us  [body(): q, g, c = (x.reshape(local, BS, width) for x in (q, g, c))]
  transfers between devices with their start and end apart: 14 -> 24, of which waited for: 11 -> 12; matrix products, arithmetic and copies ran while one was open for 16% -> 17% of each run, Pallas kernels for 0% -> 13%
where the time goes in v1:
time: 154 us; the launch traced here: 157 us
  waiting for transfers between devices  53.1 us (34%)
  Pallas kernels  38.7 us (25%)
  starting transfers between devices  28.3 us (18%)
  local copies, waits for them, and re-layouts  20.6 us (13%)
  other arithmetic  14.9 us (10%)
    pallas_call x2, Pallas kernels, attention(): pl.pallas_call(functools.partial(attention_kernel, rows, last), out_shape...  38.7 us
    ppermute x6, waiting for transfers between devices, line_sum(): up = lax.ppermute(up_term.astype(BF16), 'row', up_pairs)  25.8 us
    ppermute x6, waiting for transfers between devices, line_sum(): down = lax.ppermute(down_term.astype(BF16), 'row', down_pairs)  23.4 us
    ppermute x6, starting transfers between devices, line_sum(): down = lax.ppermute(down_term.astype(BF16), 'row', down_pairs)  14.1 us
    ppermute x6, starting transfers between devices, line_sum(): up = lax.ppermute(up_term.astype(BF16), 'row', up_pairs)  8.97 us
    convert_element_type x4, other arithmetic, line_sum(): down = lax.ppermute(down_term.astype(BF16), 'row', down_pairs)  5.56 us
    ppermute x12, starting transfers between devices, exchange(): return lax.ppermute(x, 'col', [(d, d ^ bit) for d in range(size)])  5.24 us
    dynamic_slice x2, local copies, waits for them, and re-layouts, own(): return lax.dynamic_slice_in_dim(x, start, share, 0).astype(F32)  4.73 us
  transfers between devices with their start and end apart: 24, of which 12 were waited for; matrix products, arithmetic and copies ran while one was open for 17% of the time, Pallas kernels for 13%

profile of v1, /device:TPU:18, one launch (start us, length us, event | category | flops | bytes accessed | tf_op | source)
XLA Modules:
  0.0 156.8 jit_solution(847359336440582643)
XLA Ops:
  0.7 1.0 reshape.49
  1.7 1.6 %collective-permute-start.3 = (bf16[2,128,256]{2,1,0:T(8,128)(2,1)S(1)}, bf16[2,128,256]{2,1,0:T(8,128)(2,1)S(1)}, u32[]{:S(2)}, u32[]{:S(2)}) collective-permute-start(bf16[2,128,256]{2,1,0:T(8,128)(2,1)S(1)} %reshape.49), channel_id=1, source_target_pairs={{0,4},{1,5},{2,6},{3,7},{4,0},{5,1},{6,2},{7,3},{8,12},{9,13},{10,... | collective-permute-start | bytes 393224 | tf_op jit(solution)/shard_map/ppermute | solution.py:199
  3.3 1.0 reshape.48
  4.3 0.6 collective-permute-start
  4.9 0.7 multiply_add_fusion
  5.6 0.6 slice_bitcast_fusion.2
  6.2 0.7 multiply_add_fusion.1
  6.9 0.6 slice_bitcast_fusion.3
  7.5 1.6 collective-permute-start.4
  9.0 0.3 collective-permute-done
  9.3 0.6 collective-permute-start.1
  9.9 1.3 fusion.4
  11.2 1.6 %reshape.45.refs_3_ = bf16[2,128,256]{2,1,0:T(8,128)(2,1)} reshape(bf16[256,2,128]{2,1,0:T(2,128)(2,1)} %param.8) | data formatting | bytes 262144 | tf_op jit(solution)/shard_map/reshape | solution.py:260
  12.9 0.7 reshape.46.refs_4_
  13.6 0.7 reshape.47.refs_5_
  14.4 0.6 collective-permute-done.4
  15.2 1.2 collective-permute-done.1
  16.6 0.5 collective-permute-done.5
  17.1 1.3 collective-permute-done.2
  18.4 1.0 copy-done.11
  19.4 18.9 %shard_map.119 = (bf16[128,256]{1,0:T(8,128)(2,1)}, bf16[128,256]{1,0:T(8,128)(2,1)}, bf16[8,512,256]{2,1,0:T(8,128)(2,1)}, f32[16,256,128]{2,1,0:T(8,128)}, f32[16,256,128]{2,1,0:T(8,128)}) custom-call(s32[16]{0:T(128)} %get-tuple-element.37.refs_0_, s32[16]{0:T(128)} %get-tuple-element.35.refs_1_, s32[1]{0:T(128)} %get-tuple-element.39.refs_2_, ...), custom_call_target="tpu_custom_call" | custom-call | flops 6442450944 | bytes 12582912 | tf_op jit(solution)/shard_map/pallas_call | solution.py:176
  38.3 2.3 %constant_dynamic-slice_fusion.3 = (bf16[2,512,256]{2,1,0:T(8,128)(2,1)}, bf16[2,512,256]{2,1,0:T(8,128)(2,1)}) fusion(bf16[8,512,256]{2,1,0:T(8,128)(2,1)} %get-tuple-element.23, s32[]{:T(128)S(6)} %select_n.70, s32[]{:T(128)S(6)} %select_n.73), kind=kLoop, calls=%fused_computation.36 | loop fusion | bytes 2097160 | tf_op jit(solution)/shard_map/dynamic_slice | solution.py:223
  40.6 1.3 collective-permute-start.12
  41.9 19.8 %shard_map.120 = (bf16[128,256]{1,0:T(8,128)(2,1)}, bf16[128,256]{1,0:T(8,128)(2,1)}, bf16[8,512,256]{2,1,0:T(8,128)(2,1)}, bf16[16,256,128]{2,1,0:T(8,128)(2,1)}, bf16[16,256,128]{2,1,0:T(8,128)(2,1)}) custom-call(s32[16]{0:T(128)} %get-tuple-element.38.refs_0_, s32[16]{0:T(128)} %get-tuple-element.36.refs_1_, s32[1]{0:T(128)} %get-tuple-element.40.refs_2_, ...), custom_call_target="tpu_custom_call" | custom-call | flops 6442450944 | bytes 12582912 | tf_op jit(solution)/shard_map/pallas_call | solution.py:176
  61.7 2.0 %slice.67 = bf16[8,256,128]{2,1,0:T(8,128)(2,1)} slice(bf16[16,256,128]{2,1,0:T(8,128)(2,1)} %get-tuple-element.20), slice={[8:16], [0:256], [0:128]} | slice | bytes 1048576 | tf_op jit(solution)/shard_map/slice | solution.py:211
  63.7 1.6 %collective-permute-start.15 = (bf16[2,512,256]{2,1,0:T(8,128)(2,1)}, bf16[2,512,256]{2,1,0:T(8,128)(2,1)}, u32[]{:S(2)}, u32[]{:S(2)}) collective-permute-start(bf16[2,512,256]{2,1,0:T(8,128)(2,1)} %get-tuple-element.30), channel_id=1, source_target_pairs={{0,8},{1,9},{2,10},{3,11},{4,12},{5,13},{6,14},{7,15}} | collective-permute-start | bytes 1572872 | tf_op jit(solution)/shard_map/ppermute | solution.py:235
  65.3 2.4 %constant_dynamic-slice_fusion.1 = (bf16[2,512,256]{2,1,0:T(8,128)(2,1)}, bf16[2,512,256]{2,1,0:T(8,128)(2,1)}) fusion(bf16[8,512,256]{2,1,0:T(8,128)(2,1)} %get-tuple-element.24, s32[]{:T(128)S(6)} %select_n.70, s32[]{:T(128)S(6)} %select_n.73), kind=kLoop, calls=%fused_computation.34 | loop fusion | bytes 2097160 | tf_op jit(solution)/shard_map/dynamic_slice | solution.py:223
  67.7 1.3 collective-permute-start.18
  69.1 0.7 reshape.50
  69.8 0.7 reshape.53
  70.5 0.6 collective-permute-start.6
  71.1 0.8 collective-permute-start.21
  71.9 1.2 add_convert_fusion.9
  73.1 3.1 %collective-permute-start.13 = (bf16[2,512,256]{2,1,0:T(8,128)(2,1)S(1)}, bf16[2,512,256]{2,1,0:T(8,128)(2,1)S(1)}, u32[]{:S(2)}, u32[]{:S(2)}) collective-permute-start(bf16[2,512,256]{2,1,0:T(8,128)(2,1)S(1)} %add_convert_fusion.9), channel_id=1, source_target_pairs={{16,8},{24,16},{17,9},{25,17},{18,10},{26,18},{19,11},{27,19},{20,... | collective-permute-start | bytes 1572872 | tf_op jit(solution)/shard_map/ppermute | solution.py:234
  76.3 1.2 add_convert_fusion.10
  77.5 8.1 %collective-permute-done.18 = bf16[2,512,256]{2,1,0:T(8,128)(2,1)} collective-permute-done((bf16[2,512,256]{2,1,0:T(8,128)(2,1)}, bf16[2,512,256]{2,1,0:T(8,128)(2,1)}, u32[]{:S(2)}, u32[]{:S(2)}) %collective-permute-start.18) | collective-permute-done | bytes 524320 | tf_op jit(solution)/shard_map/ppermute | solution.py:234
  85.5 1.2 add_convert_fusion.4
  86.7 1.9 %collective-permute-start.19 = (bf16[2,512,256]{2,1,0:T(8,128)(2,1)S(1)}, bf16[2,512,256]{2,1,0:T(8,128)(2,1)S(1)}, u32[]{:S(2)}, u32[]{:S(2)}) collective-permute-start(bf16[2,512,256]{2,1,0:T(8,128)(2,1)S(1)} %add_convert_fusion.4), channel_id=1, source_target_pairs={{16,8},{24,16},{17,9},{25,17},{18,10},{26,18},{19,11},{27,19},{20,... | collective-permute-start | bytes 1572872 | tf_op jit(solution)/shard_map/ppermute | solution.py:234
  88.7 0.1 add_convert_fusion.11
  88.9 7.7 %collective-permute-done.13 = bf16[2,512,256]{2,1,0:T(8,128)(2,1)S(1)} collective-permute-done((bf16[2,512,256]{2,1,0:T(8,128)(2,1)S(1)}, bf16[2,512,256]{2,1,0:T(8,128)(2,1)S(1)}, u32[]{:S(2)}, u32[]{:S(2)}) %collective-permute-start.13) | collective-permute-done | bytes 524320 | tf_op jit(solution)/shard_map/ppermute | solution.py:234
  96.7 2.1 %add_convert_fusion.8 = (bf16[2,512,256]{2,1,0:T(8,128)(2,1)}, bf16[2,512,256]{2,1,0:T(8,128)(2,1)S(1)}) fusion(bf16[2,512,256]{2,1,0:T(8,128)(2,1)S(1)} %collective-permute-done.13, bf16[8,512,256]{2,1,0:T(8,128)(2,1)S(1)} %copy-done, s32[]{:T(128)S(6)} %select_n.68, bf16[2,512,256]{2,1,0:T(8,128)(2,1)} %collective-permute-done.15, s32[]{:T(128)S(6)} %select_n.72), kind=kLoop, calls=%fused_computation.9 | loop fusion | flops 2097152 | bytes 3145736 | tf_op jit(solution)/shard_map/convert_element_type | solution.py:234
  98.8 1.3 collective-permute-start.16
  100.1 7.6 %collective-permute-done.19 = bf16[2,512,256]{2,1,0:T(8,128)(2,1)S(1)} collective-permute-done((bf16[2,512,256]{2,1,0:T(8,128)(2,1)S(1)}, bf16[2,512,256]{2,1,0:T(8,128)(2,1)S(1)}, u32[]{:S(2)}, u32[]{:S(2)}) %collective-permute-start.19) | collective-permute-done | bytes 524320 | tf_op jit(solution)/shard_map/ppermute | solution.py:234
  107.7 1.1 add_convert_fusion.3
  108.8 1.3 collective-permute-start.22
  110.4 4.6 %collective-permute-start.14 = (bf16[2,512,256]{2,1,0:T(8,128)(2,1)}, bf16[2,512,256]{2,1,0:T(8,128)(2,1)}, u32[]{:S(2)}, u32[]{:S(2)}) collective-permute-start(bf16[2,512,256]{2,1,0:T(8,128)(2,1)} %get-tuple-element.27), channel_id=1, source_target_pairs={{8,0},{16,8},{24,16},{9,1},{17,9},{25,17},{10,2},{18,10},{26,18},{... | collective-permute-start | bytes 1572872 | tf_op jit(solution)/shard_map/ppermute | solution.py:234
  115.0 0.2 collective-permute-done.16
  115.2 1.9 %collective-permute-start.20 = (bf16[2,512,256]{2,1,0:T(8,128)(2,1)}, bf16[2,512,256]{2,1,0:T(8,128)(2,1)S(1)}, u32[]{:S(2)}, u32[]{:S(2)}) collective-permute-start(bf16[2,512,256]{2,1,0:T(8,128)(2,1)} %get-tuple-element.31), channel_id=1, source_target_pairs={{8,0},{16,8},{24,16},{9,1},{17,9},{25,17},{10,2},{18,10},{26,18},{... | collective-permute-start | bytes 1572872 | tf_op jit(solution)/shard_map/ppermute | solution.py:234
  117.1 1.0 add_convert_fusion.6
  118.1 7.3 %collective-permute-done.22 = bf16[2,512,256]{2,1,0:T(8,128)(2,1)S(1)} collective-permute-done((bf16[2,512,256]{2,1,0:T(8,128)(2,1)S(1)}, bf16[2,512,256]{2,1,0:T(8,128)(2,1)S(1)}, u32[]{:S(2)}, u32[]{:S(2)}) %collective-permute-start.22) | collective-permute-done | bytes 524320 | tf_op jit(solution)/shard_map/ppermute | solution.py:235
  125.5 1.9 %collective-permute-start.17 = (bf16[2,512,256]{2,1,0:T(8,128)(2,1)}, bf16[2,512,256]{2,1,0:T(8,128)(2,1)}, u32[]{:S(2)}, u32[]{:S(2)}) collective-permute-start(bf16[2,512,256]{2,1,0:T(8,128)(2,1)} %add_convert_fusion.6), channel_id=1, source_target_pairs={{0,8},{8,16},{16,24},{1,9},{9,17},{17,25},{2,10},{10,18},{18,26},{... | collective-permute-start | bytes 1572872 | tf_op jit(solution)/shard_map/ppermute | solution.py:235
  127.4 1.0 add_convert_fusion.1
  128.4 2.1 %collective-permute-start.23 = (bf16[2,512,256]{2,1,0:T(8,128)(2,1)}, bf16[2,512,256]{2,1,0:T(8,128)(2,1)}, u32[]{:S(2)}, u32[]{:S(2)}) collective-permute-start(bf16[2,512,256]{2,1,0:T(8,128)(2,1)} %add_convert_fusion.1), channel_id=1, source_target_pairs={{0,8},{8,16},{16,24},{1,9},{9,17},{17,25},{2,10},{10,18},{18,26},{... | collective-permute-start | bytes 1572872 | tf_op jit(solution)/shard_map/ppermute | solution.py:235
  130.6 0.7 reshape.52
  131.4 0.1 copy.14
  131.5 0.7 reshape.51
  132.2 10.4 %collective-permute-done.17 = bf16[2,512,256]{2,1,0:T(8,128)(2,1)} collective-permute-done((bf16[2,512,256]{2,1,0:T(8,128)(2,1)}, bf16[2,512,256]{2,1,0:T(8,128)(2,1)}, u32[]{:S(2)}, u32[]{:S(2)}) %collective-permute-start.17) | collective-permute-done | bytes 524320 | tf_op jit(solution)/shard_map/ppermute | solution.py:235
  142.5 1.4 add_convert_fusion.5
  143.9 0.1 stack.9
  144.1 7.9 %collective-permute-done.23 = bf16[2,512,256]{2,1,0:T(8,128)(2,1)} collective-permute-done((bf16[2,512,256]{2,1,0:T(8,128)(2,1)}, bf16[2,512,256]{2,1,0:T(8,128)(2,1)}, u32[]{:S(2)}, u32[]{:S(2)}) %collective-permute-start.23) | collective-permute-done | bytes 524320 | tf_op jit(solution)/shard_map/ppermute | solution.py:235
  152.0 1.4 add_convert_fusion
  153.4 0.1 stack.10
  153.5 1.5 maximum_bitcast_fusion
  155.0 1.8 %copy.16 = bf16[2,4,128,2,2,128]{5,4,3,2,1,0:T(2,128)(2,1)} copy(bf16[2,4,128,2,2,128]{5,4,2,1,3,0:T(2,128)(2,1)S(1)} %maximum_bitcast_fusion) | data formatting | bytes 2097152 | tf_op jit(solution)/shard_map/transpose | solution.py:280
  (65 shorter events, 1.2 us)
Async XLA Ops:
  0.6 12.3 %copy-start.4 = (bf16[256,2,128]{2,1,0:T(2,128)(2,1)S(1)}, bf16[256,2,128]{2,1,0:T(2,128)(2,1)}, u32[]{:S(2)}) copy-start(bf16[256,2,128]{2,1,0:T(2,128)(2,1)} %param.11) | copy-start | bytes 393220
  0.6 13.0 %copy-start.5 = (bf16[256,2,128]{2,1,0:T(2,128)(2,1)S(1)}, bf16[256,2,128]{2,1,0:T(2,128)(2,1)}, u32[]{:S(2)}) copy-start(bf16[256,2,128]{2,1,0:T(2,128)(2,1)} %param.12) | copy-start | bytes 393220
  1.7 5.7 %collective-permute-start.3 = (bf16[2,128,256]{2,1,0:T(8,128)(2,1)S(1)}, bf16[2,128,256]{2,1,0:T(8,128)(2,1)S(1)}, u32[]{:S(2)}, u32[]{:S(2)}) collective-permute-start(bf16[2,128,256]{2,1,0:T(8,128)(2,1)S(1)} %reshape.49), channel_id=1, source_target_pairs={{0,4},{1,5},{2,6},{3,7},{4,0},{5,1},{6,2},{7,3},{8,12},{9,13},{10,... | collective-permute-start | bytes 393224 | tf_op jit(solution)/shard_map/ppermute | solution.py:199
  4.3 5.0 %collective-permute-start = (bf16[2,128,256]{2,1,0:T(8,128)(2,1)S(1)}, bf16[2,128,256]{2,1,0:T(8,128)(2,1)S(1)}, u32[]{:S(2)}, u32[]{:S(2)}) collective-permute-start(bf16[2,128,256]{2,1,0:T(8,128)(2,1)S(1)} %reshape.48), channel_id=1, source_target_pairs={{0,2},{1,3},{2,0},{3,1},{4,6},{5,7},{6,4},{7,5},{8,10},{9,11},{10,... | collective-permute-start | bytes 393224 | tf_op jit(solution)/shard_map/ppermute | solution.py:199
  7.5 7.6 %collective-permute-start.4 = (bf16[4,128,256]{2,1,0:T(8,128)(2,1)S(1)}, bf16[4,128,256]{2,1,0:T(8,128)(2,1)S(1)}, u32[]{:S(2)}, u32[]{:S(2)}) collective-permute-start(bf16[4,128,256]{2,1,0:T(8,128)(2,1)S(1)} %pad_maximum_fusion.3), channel_id=1, source_target_pairs={{0,2},{1,3},{2,0},{3,1},{4,6},{5,7},{6,4},{7,5},{8,10},{9,11},{10,... | collective-permute-start | bytes 786440 | tf_op jit(solution)/shard_map/ppermute | solution.py:199
  9.3 7.0 %collective-permute-start.1 = (bf16[4,128,256]{2,1,0:T(8,128)(2,1)S(1)}, bf16[4,128,256]{2,1,0:T(8,128)(2,1)S(1)}, u32[]{:S(2)}, u32[]{:S(2)}) collective-permute-start(bf16[4,128,256]{2,1,0:T(8,128)(2,1)S(1)} %pad_maximum_fusion.2), channel_id=1, source_target_pairs={{0,4},{1,5},{2,6},{3,7},{4,0},{5,1},{6,2},{7,3},{8,12},{9,13},{10,... | collective-permute-start | bytes 786440 | tf_op jit(solution)/shard_map/ppermute | solution.py:199
  15.1 2.0 %collective-permute-start.5 = (bf16[8,128,256]{2,1,0:T(8,128)(2,1)S(1)}, bf16[8,128,256]{2,1,0:T(8,128)(2,1)S(1)}, u32[]{:S(2)}, u32[]{:S(2)}) collective-permute-start(bf16[8,128,256]{2,1,0:T(8,128)(2,1)S(1)} %pad_maximum_fusion.1), channel_id=1, source_target_pairs={{0,1},{1,0},{2,3},{3,2},{4,5},{5,4},{6,7},{7,6},{8,9},{9,8},{10,11... | collective-permute-start | bytes 1572872 | tf_op jit(solution)/shard_map/ppermute | solution.py:199
  16.4 2.0 %collective-permute-start.2 = (bf16[8,128,256]{2,1,0:T(8,128)(2,1)S(1)}, bf16[8,128,256]{2,1,0:T(8,128)(2,1)S(1)}, u32[]{:S(2)}, u32[]{:S(2)}) collective-permute-start(bf16[8,128,256]{2,1,0:T(8,128)(2,1)S(1)} %pad_maximum_fusion), channel_id=1, source_target_pairs={{0,1},{1,0},{2,3},{3,2},{4,5},{5,4},{6,7},{7,6},{8,9},{9,8},{10,11... | collective-permute-start | bytes 1572872 | tf_op jit(solution)/shard_map/ppermute | solution.py:199
  17.1 1.3 copy-start.10
  18.4 1.0 copy-start.11
  40.6 30.5 %collective-permute-start.12 = (bf16[2,512,256]{2,1,0:T(8,128)(2,1)}, bf16[2,512,256]{2,1,0:T(8,128)(2,1)}, u32[]{:S(2)}, u32[]{:S(2)}) collective-permute-start(bf16[2,512,256]{2,1,0:T(8,128)(2,1)} %get-tuple-element.29), channel_id=1, source_target_pairs={{24,16},{25,17},{26,18},{27,19},{28,20},{29,21},{30,22},{31,23}} | collective-permute-start | bytes 1572872 | tf_op jit(solution)/shard_map/ppermute | solution.py:234
  61.7 7.3 %copy-start.6 = (bf16[128,256]{1,0:T(8,128)(2,1)S(1)}, bf16[128,256]{1,0:T(8,128)(2,1)}, u32[]{:S(2)}) copy-start(bf16[128,256]{1,0:T(8,128)(2,1)} %get-tuple-element.15) | copy-start | bytes 196612
  61.7 7.3 %copy-start.7 = (bf16[128,256]{1,0:T(8,128)(2,1)S(1)}, bf16[128,256]{1,0:T(8,128)(2,1)}, u32[]{:S(2)}) copy-start(bf16[128,256]{1,0:T(8,128)(2,1)} %get-tuple-element.21) | copy-start | bytes 196612
  61.7 8.8 %copy-start.2 = (bf16[16,256,128]{2,1,0:T(8,128)(2,1)S(1)}, bf16[16,256,128]{2,1,0:T(8,128)(2,1)}, u32[]{:S(2)}) copy-start(bf16[16,256,128]{2,1,0:T(8,128)(2,1)} %get-tuple-element.19) | copy-start | bytes 3145732
  63.7 9.4 %collective-permute-start.9 = (bf16[8,256,128]{2,1,0:T(8,128)(2,1)}, bf16[8,256,128]{2,1,0:T(8,128)(2,1)}, u32[]{:S(2)}, u32[]{:S(2)}) collective-permute-start(bf16[8,256,128]{2,1,0:T(8,128)(2,1)} %slice.67), channel_id=1, source_target_pairs={{0,1},{1,0},{2,3},{3,2},{4,5},{5,4},{6,7},{7,6},{8,9},{9,8},{10,11... | collective-permute-start | bytes 1572872 | tf_op jit(solution)/shard_map/ppermute | solution.py:199
  63.7 5.3 %copy-start.8 = (bf16[128,256]{1,0:T(8,128)(2,1)S(1)}, bf16[128,256]{1,0:T(8,128)(2,1)}, u32[]{:S(2)}) copy-start(bf16[128,256]{1,0:T(8,128)(2,1)} %get-tuple-element.18) | copy-start | bytes 196612
  63.7 5.3 %copy-start.9 = (bf16[128,256]{1,0:T(8,128)(2,1)S(1)}, bf16[128,256]{1,0:T(8,128)(2,1)}, u32[]{:S(2)}) copy-start(bf16[128,256]{1,0:T(8,128)(2,1)} %get-tuple-element.22) | copy-start | bytes 196612
  63.7 25.1 %collective-permute-start.15 = (bf16[2,512,256]{2,1,0:T(8,128)(2,1)}, bf16[2,512,256]{2,1,0:T(8,128)(2,1)}, u32[]{:S(2)}, u32[]{:S(2)}) collective-permute-start(bf16[2,512,256]{2,1,0:T(8,128)(2,1)} %get-tuple-element.30), channel_id=1, source_target_pairs={{0,8},{1,9},{2,10},{3,11},{4,12},{5,13},{6,14},{7,15}} | collective-permute-start | bytes 1572872 | tf_op jit(solution)/shard_map/ppermute | solution.py:235
  65.3 6.6 %copy-start = (bf16[8,512,256]{2,1,0:T(8,128)(2,1)S(1)}, bf16[8,512,256]{2,1,0:T(8,128)(2,1)}, u32[]{:S(2)}) copy-start(bf16[8,512,256]{2,1,0:T(8,128)(2,1)} %get-tuple-element.23) | copy-start | bytes 6291460
  67.7 17.8 %collective-permute-start.18 = (bf16[2,512,256]{2,1,0:T(8,128)(2,1)}, bf16[2,512,256]{2,1,0:T(8,128)(2,1)}, u32[]{:S(2)}, u32[]{:S(2)}) collective-permute-start(bf16[2,512,256]{2,1,0:T(8,128)(2,1)} %get-tuple-element.33), channel_id=1, source_target_pairs={{24,16},{25,17},{26,18},{27,19},{28,20},{29,21},{30,22},{31,23}} | collective-permute-start | bytes 1572872 | tf_op jit(solution)/shard_map/ppermute | solution.py:234
  70.5 5.8 %copy-start.3 = (bf16[16,256,128]{2,1,0:T(8,128)(2,1)S(1)}, bf16[16,256,128]{2,1,0:T(8,128)(2,1)}, u32[]{:S(2)}) copy-start(bf16[16,256,128]{2,1,0:T(8,128)(2,1)} %get-tuple-element.20) | copy-start | bytes 3145732
  70.5 15.0 %copy-start.1 = (bf16[8,512,256]{2,1,0:T(8,128)(2,1)S(1)}, bf16[8,512,256]{2,1,0:T(8,128)(2,1)}, u32[]{:S(2)}) copy-start(bf16[8,512,256]{2,1,0:T(8,128)(2,1)} %get-tuple-element.24) | copy-start | bytes 6291460
  70.5 16.2 %collective-permute-start.6 = (bf16[8,256,128]{2,1,0:T(8,128)(2,1)S(1)}, bf16[8,256,128]{2,1,0:T(8,128)(2,1)S(1)}, u32[]{:S(2)}, u32[]{:S(2)}) collective-permute-start(bf16[8,256,128]{2,1,0:T(8,128)(2,1)S(1)} %slice.61), channel_id=1, source_target_pairs={{0,1},{1,0},{2,3},{3,2},{4,5},{5,4},{6,7},{7,6},{8,9},{9,8},{10,11... | collective-permute-start | bytes 1572872 | tf_op jit(solution)/shard_map/ppermute | solution.py:199
  71.1 29.0 %collective-permute-start.21 = (bf16[2,512,256]{2,1,0:T(8,128)(2,1)}, bf16[2,512,256]{2,1,0:T(8,128)(2,1)S(1)}, u32[]{:S(2)}, u32[]{:S(2)}) collective-permute-start(bf16[2,512,256]{2,1,0:T(8,128)(2,1)} %get-tuple-element.34), channel_id=1, source_target_pairs={{0,8},{1,9},{2,10},{3,11},{4,12},{5,13},{6,14},{7,15}} | collective-permute-start | bytes 1572872 | tf_op jit(solution)/shard_map/ppermute | solution.py:235
  73.1 23.5 %collective-permute-start.13 = (bf16[2,512,256]{2,1,0:T(8,128)(2,1)S(1)}, bf16[2,512,256]{2,1,0:T(8,128)(2,1)S(1)}, u32[]{:S(2)}, u32[]{:S(2)}) collective-permute-start(bf16[2,512,256]{2,1,0:T(8,128)(2,1)S(1)} %add_convert_fusion.9), channel_id=1, source_target_pairs={{16,8},{24,16},{17,9},{25,17},{18,10},{26,18},{19,11},{27,19},{20,... | collective-permute-start | bytes 1572872 | tf_op jit(solution)/shard_map/ppermute | solution.py:234
  85.5 24.5 %collective-permute-start.10 = (bf16[4,256,128]{2,1,0:T(8,128)(2,1)S(1)}, bf16[4,256,128]{2,1,0:T(8,128)(2,1)S(1)}, u32[]{:S(2)}, u32[]{:S(2)}) collective-permute-start(bf16[4,256,128]{2,1,0:T(8,128)(2,1)S(1)} %slice.77), channel_id=1, source_target_pairs={{0,2},{1,3},{2,0},{3,1},{4,6},{5,7},{6,4},{7,5},{8,10},{9,11},{10,... | collective-permute-start | bytes 786440 | tf_op jit(solution)/shard_map/ppermute | solution.py:199
  86.7 21.0 %collective-permute-start.19 = (bf16[2,512,256]{2,1,0:T(8,128)(2,1)S(1)}, bf16[2,512,256]{2,1,0:T(8,128)(2,1)S(1)}, u32[]{:S(2)}, u32[]{:S(2)}) collective-permute-start(bf16[2,512,256]{2,1,0:T(8,128)(2,1)S(1)} %add_convert_fusion.4), channel_id=1, source_target_pairs={{16,8},{24,16},{17,9},{25,17},{18,10},{26,18},{19,11},{27,19},{20,... | collective-permute-start | bytes 1572872 | tf_op jit(solution)/shard_map/ppermute | solution.py:234
  88.9 21.4 %collective-permute-start.7 = (bf16[4,256,128]{2,1,0:T(8,128)(2,1)S(1)}, bf16[4,256,128]{2,1,0:T(8,128)(2,1)S(1)}, u32[]{:S(2)}, u32[]{:S(2)}) collective-permute-start(bf16[4,256,128]{2,1,0:T(8,128)(2,1)S(1)} %slice.73), channel_id=1, source_target_pairs={{0,4},{1,5},{2,6},{3,7},{4,0},{5,1},{6,2},{7,3},{8,12},{9,13},{10,... | collective-permute-start | bytes 786440 | tf_op jit(solution)/shard_map/ppermute | solution.py:199
  98.8 16.4 %collective-permute-start.16 = (bf16[2,512,256]{2,1,0:T(8,128)(2,1)S(1)}, bf16[2,512,256]{2,1,0:T(8,128)(2,1)S(1)}, u32[]{:S(2)}, u32[]{:S(2)}) collective-permute-start(bf16[2,512,256]{2,1,0:T(8,128)(2,1)S(1)} %get-tuple-element.28), channel_id=1, source_target_pairs={{0,8},{8,16},{1,9},{9,17},{2,10},{10,18},{3,11},{11,19},{4,12},{12... | collective-permute-start | bytes 1572872 | tf_op jit(solution)/shard_map/ppermute | solution.py:235
  108.8 16.7 %collective-permute-start.22 = (bf16[2,512,256]{2,1,0:T(8,128)(2,1)S(1)}, bf16[2,512,256]{2,1,0:T(8,128)(2,1)S(1)}, u32[]{:S(2)}, u32[]{:S(2)}) collective-permute-start(bf16[2,512,256]{2,1,0:T(8,128)(2,1)S(1)} %get-tuple-element.32), channel_id=1, source_target_pairs={{0,8},{8,16},{1,9},{9,17},{2,10},{10,18},{3,11},{11,19},{4,12},{12... | collective-permute-start | bytes 1572872 | tf_op jit(solution)/shard_map/ppermute | solution.py:235
  110.2 18.2 %collective-permute-start.11 = (bf16[2,256,128]{2,1,0:T(8,128)(2,1)S(1)}, bf16[2,256,128]{2,1,0:T(8,128)(2,1)S(1)}, u32[]{:S(2)}, u32[]{:S(2)}) collective-permute-start(bf16[2,256,128]{2,1,0:T(8,128)(2,1)S(1)} %slice.79), channel_id=1, source_target_pairs={{0,4},{1,5},{2,6},{3,7},{4,0},{5,1},{6,2},{7,3},{8,12},{9,13},{10,... | collective-permute-start | bytes 393224 | tf_op jit(solution)/shard_map/ppermute | solution.py:199
  110.4 20.9 %collective-permute-start.8 = (bf16[2,256,128]{2,1,0:T(8,128)(2,1)S(1)}, bf16[2,256,128]{2,1,0:T(8,128)(2,1)S(1)}, u32[]{:S(2)}, u32[]{:S(2)}) collective-permute-start(bf16[2,256,128]{2,1,0:T(8,128)(2,1)S(1)} %slice.75), channel_id=1, source_target_pairs={{0,2},{1,3},{2,0},{3,1},{4,6},{5,7},{6,4},{7,5},{8,10},{9,11},{10,... | collective-permute-start | bytes 393224 | tf_op jit(solution)/shard_map/ppermute | solution.py:199
  110.4 21.7 %collective-permute-start.14 = (bf16[2,512,256]{2,1,0:T(8,128)(2,1)}, bf16[2,512,256]{2,1,0:T(8,128)(2,1)}, u32[]{:S(2)}, u32[]{:S(2)}) collective-permute-start(bf16[2,512,256]{2,1,0:T(8,128)(2,1)} %get-tuple-element.27), channel_id=1, source_target_pairs={{8,0},{16,8},{24,16},{9,1},{17,9},{25,17},{10,2},{18,10},{26,18},{... | collective-permute-start | bytes 1572872 | tf_op jit(solution)/shard_map/ppermute | solution.py:234
  115.2 28.8 %collective-permute-start.20 = (bf16[2,512,256]{2,1,0:T(8,128)(2,1)}, bf16[2,512,256]{2,1,0:T(8,128)(2,1)S(1)}, u32[]{:S(2)}, u32[]{:S(2)}) collective-permute-start(bf16[2,512,256]{2,1,0:T(8,128)(2,1)} %get-tuple-element.31), channel_id=1, source_target_pairs={{8,0},{16,8},{24,16},{9,1},{17,9},{25,17},{10,2},{18,10},{26,18},{... | collective-permute-start | bytes 1572872 | tf_op jit(solution)/shard_map/ppermute | solution.py:234
  125.5 17.1 %collective-permute-start.17 = (bf16[2,512,256]{2,1,0:T(8,128)(2,1)}, bf16[2,512,256]{2,1,0:T(8,128)(2,1)}, u32[]{:S(2)}, u32[]{:S(2)}) collective-permute-start(bf16[2,512,256]{2,1,0:T(8,128)(2,1)} %add_convert_fusion.6), channel_id=1, source_target_pairs={{0,8},{8,16},{16,24},{1,9},{9,17},{17,25},{2,10},{10,18},{18,26},{... | collective-permute-start | bytes 1572872 | tf_op jit(solution)/shard_map/ppermute | solution.py:235
  128.4 23.6 %collective-permute-start.23 = (bf16[2,512,256]{2,1,0:T(8,128)(2,1)}, bf16[2,512,256]{2,1,0:T(8,128)(2,1)}, u32[]{:S(2)}, u32[]{:S(2)}) collective-permute-start(bf16[2,512,256]{2,1,0:T(8,128)(2,1)} %add_convert_fusion.1), channel_id=1, source_target_pairs={{0,8},{8,16},{16,24},{1,9},{9,17},{17,25},{2,10},{10,18},{18,26},{... | collective-permute-start | bytes 1572872 | tf_op jit(solution)/shard_map/ppermute | solution.py:235
